TPU v7x, 32 devices: a whole 2x2x4 slice. The times are simulated.
32 devices in a mesh: parts: 2 (over y), row: 4 (over z), col: 2 (over x), cores: 2 (over core).
Axes of the slice: x: 2, y: 2, z: 4, core: 2. Of those that a mesh axis runs over, the one named last changes fastest.
Arguments:
- latent: float32 [128, 256, 128], P(('parts', 'row', 'cores'), 'col'), parts along dimension 0, may hold values from -6 to 6
- moment_one: float32 [128, 256, 128], P(('parts', 'row', 'cores'), 'col'), parts along dimension 0, may hold values from -0.3 to 0.3
- moment_two: float32 [128, 256, 128], P(('parts', 'row', 'cores'), 'col'), parts along dimension 0, may hold values from 0.001 to 0.01
- hole_mask: int32 [128, 256], P(('parts', 'row', 'cores'), 'col'), parts along dimension 0, may hold values 0 or 1
- target_rgb: float32 [3, 128, 256], P(None, ('parts', 'row', 'cores'), 'col'), parts along dimension 1, may hold values from -4 to 4
- kernel_one: bfloat16 [3, 3, 128, 128], replicated, may hold values from -0.1875 to 0.1875
- bias_one: float32 [128], replicated, may hold values from -3 to 3
- kernel_two: bfloat16 [3, 3, 128, 128], replicated, may hold values from -0.1875 to 0.1875
- bias_two: float32 [128], replicated, may hold values from -3 to 3
- rgb_weight: bfloat16 [3, 128], replicated, may hold values from -0.5 to 0.5
Outputs:
- latent_out: float32 [128, 256, 128], P(('parts', 'row', 'cores'), 'col'), parts along dimension 0
- moment_one_out: float32 [128, 256, 128], P(('parts', 'row', 'cores'), 'col'), parts along dimension 0
- moment_two_out: float32 [128, 256, 128], P(('parts', 'row', 'cores'), 'col'), parts along dimension 0
There are 2 independent parts, one for each index of `parts`. A program takes and returns all parts, laid end to end along the dimension named above; an argument that names none is the same for every part. Nothing has to cross between parts.
All inputs are finite; a program needn't handle non-finite values. No bound on the sum of `hole_mask` on one device may be relied on, other than what follows from the above.
Results may differ from a plain program's by a relative error of at most 0.0045.
Values may be sent and summed in bfloat16 or wider, within the bound.
A program may use at most 64 MiB of HBM per device.

v0:
```python
import functools

import jax
import jax.numpy as jnp
from jax import lax
from jax.experimental import pallas as pl
from jax.experimental.pallas import tpu as pltpu
from jax.sharding import PartitionSpec as P

STEPS = 2
BETA_ONE = 0.6
BETA_TWO = 0.9
LEARN_RATE = 0.4
EPSILON = 1e-08

MESH = pl.DeviceIdType.MESH
HALO = 4
WRAP = 16
DIRS = [(-1, 0), (1, 0), (0, -1), (0, 1), (-1, -1), (-1, 1), (1, -1), (1, 1)]


def sweep(product, finish, places):
    ready = product(places[0])
    for at, q in enumerate(places):
        held = ready
        if at + 1 < len(places):
            ready = product(places[at + 1])
        finish(q, held)


def kernel(
    height,
    breadth,
    rows_n,
    cols_n,
    cores_n,
    latent_hbm,
    one_hbm,
    two_hbm,
    mask_hbm,
    target_hbm,
    kone_hbm,
    ktwo_hbm,
    bone_ref,
    btwo_ref,
    rgb_ref,
    latent_out,
    one_out,
    two_out,
    grad_out,
    z_ref,
    m_ref,
    v_ref,
    grad_ref,
    maski,
    aux,
    aux_in,
    stage,
    row_in,
    col_in,
    diag_in,
    zx,
    h1,
    g2,
    g1,
    slope1,
    weights,
    wide,
    rgb_f,
    rgb_t,
    rgb_b,
    target_p,
    target_t,
    mask_t,
    local_sem,
    out_sem,
    send_sem,
    recv_sem,
    aux_send,
    aux_recv,
):
    width = breadth + WRAP
    place = lax.axis_index("row") * cores_n + lax.axis_index("cores")
    col = lax.axis_index("col")
    ranks = rows_n * cores_n

    def there(d):
        dr, dc = d
        ok = None
        if dr:
            ok = place > 0 if dr < 0 else place < ranks - 1
        if dc:
            side = col > 0 if dc < 0 else col < cols_n - 1
            ok = side if ok is None else jnp.logical_and(ok, side)
        return ok

    def peer(d):
        spot = place + d[0]
        return {
            "row": spot // cores_n,
            "cores": lax.rem(spot, cores_n),
            "col": col + d[1],
        }

    live = [d for d in DIRS if not (d[1] and cols_n == 1) and not (d[0] and ranks == 1)]
    slot = {d: i for i, d in enumerate(DIRS)}

    def back(d):
        return (-d[0], -d[1])

    def local(src, dst, i):
        return pltpu.make_async_copy(src, dst, local_sem.at[i])

    loads = [
        local(latent_hbm, z_ref, 0),
        local(target_hbm, aux.at[pl.ds(0, 3)], 1),
        local(mask_hbm, maski, 2),
        local(ktwo_hbm, weights.at[1, pl.ds(0, 9 * 128), pl.ds(0, 128)], 3),
        local(kone_hbm, weights.at[0, pl.ds(0, 9 * 128), pl.ds(0, 128)], 4),
        local(kone_hbm, weights.at[0, pl.ds(384, 9 * 128), pl.ds(128, 128)], 5),
        local(ktwo_hbm, weights.at[1, pl.ds(384, 9 * 128), pl.ds(128, 128)], 6),
        local(one_hbm, m_ref, 7),
        local(two_hbm, v_ref, 8),
    ]
    for c in loads:
        c.start()

    barrier = pltpu.get_barrier_semaphore()
    for d in live:

        @pl.when(there(d))
        def _():
            pl.semaphore_signal(barrier, inc=1, device_id=peer(d), device_id_type=MESH)

    def landing(d, step):
        if d[1] == 0:
            return row_in.at[step, 0 if d[0] < 0 else 1]
        if d[0] == 0:
            return col_in.at[step, 0 if d[1] < 0 else 1]
        return diag_in.at[step, 0 if d[0] < 0 else 1, 0 if d[1] < 0 else 1]

    def outgoing(d, step):
        rows = {0: pl.ds(0, height), -1: pl.ds(0, HALO), 1: pl.ds(height - HALO, HALO)}[d[0]]
        cols = {0: pl.ds(0, breadth), -1: pl.ds(0, WRAP), 1: pl.ds(breadth - WRAP, WRAP)}[d[1]]
        return stage.at[step, rows, cols]

    def halo_copy(d, step):
        return pltpu.make_async_remote_copy(
            src_ref=outgoing(d, step),
            dst_ref=landing(back(d), step),
            send_sem=send_sem.at[step, slot[d]],
            recv_sem=recv_sem.at[step, slot[back(d)]],
            device_id=peer(d),
            device_id_type=MESH,
        )

    def halo_arrival(d, step):
        return pltpu.make_async_remote_copy(
            src_ref=outgoing(back(d), step),
            dst_ref=landing(d, step),
            send_sem=send_sem.at[step, slot[back(d)]],
            recv_sem=recv_sem.at[step, slot[d]],
            device_id=peer(d),
            device_id_type=MESH,
        )

    def aux_copy(d):
        return pltpu.make_async_remote_copy(
            src_ref=aux,
            dst_ref=aux_in.at[slot[back(d)]],
            send_sem=aux_send.at[slot[d]],
            recv_sem=aux_recv.at[slot[back(d)]],
            device_id=peer(d),
            device_id_type=MESH,
        )

    def aux_arrival(d):
        return pltpu.make_async_remote_copy(
            src_ref=aux,
            dst_ref=aux_in.at[slot[d]],
            send_sem=aux_send.at[slot[back(d)]],
            recv_sem=aux_recv.at[slot[d]],
            device_id=peer(d),
            device_id_type=MESH,
        )

    def for_each(dirs, fn):
        for d in dirs:
            if d in live:

                @pl.when(there(d))
                def _():
                    fn(d)

    def clear(d):
        for step in range(STEPS):
            ref = landing(d, step)
            ref[...] = jnp.zeros(ref.shape, ref.dtype)
        aux_in[slot[d]] = jnp.zeros(aux_in.shape[1:], aux_in.dtype)

    for d in DIRS:
        if d not in live:
            clear(d)
        else:

            @pl.when(jnp.logical_not(there(d)))
            def _():
                clear(d)

    sides = [d for d in DIRS if d[0] == 0]
    verticals = [d for d in DIRS if d[0] != 0]
    uppers = [d for d in DIRS if d[0] < 0]
    lowers = [d for d in DIRS if d[0] > 0]

    loads[0].wait()
    stage[0] = z_ref[...].astype(jnp.bfloat16)
    peers = jnp.int32(0)
    for d in live:
        peers = peers + there(d).astype(jnp.int32)
    pl.semaphore_wait(barrier, peers)

    for_each(verticals + sides, lambda d: halo_copy(d, 0).start())
    loads[1].wait()
    loads[2].wait()
    aux[3] = maski[...].astype(jnp.float32)
    for_each(DIRS, lambda d: aux_copy(d).start())

    zero_block = jnp.zeros((384, 128), jnp.bfloat16)
    for i in range(4):
        weights[i, pl.ds(9 * 128, 384), pl.ds(0, 128)] = zero_block
        weights[i, pl.ds(0, 384), pl.ds(128, 128)] = zero_block
    for i in range(3, 7):
        loads[i].wait()

    def turned(layer):
        def flip(tap, carry):
            block = weights[layer, pl.ds(pl.multiple_of(tap * 128, 128), 128), pl.ds(0, 128)]
            block = block.astype(jnp.float32).T.astype(jnp.bfloat16)
            spot = pl.multiple_of((8 - tap) * 128, 128)
            weights[2 + layer, pl.ds(spot, 128), pl.ds(0, 128)] = block
            weights[2 + layer, pl.ds(pl.multiple_of(spot + 384, 128), 128), pl.ds(128, 128)] = block
            return carry

        lax.fori_loop(0, 9, flip, 0)

    turned(1)
    turned(0)

    rgb_f[...] = jnp.zeros(rgb_f.shape, jnp.float32)
    projection = rgb_ref[...].astype(jnp.float32)
    rgb_f[pl.ds(0, 3), pl.ds(0, 128)] = projection
    rgb_f[pl.ds(3, 3), pl.ds(128, 128)] = projection
    full = rgb_f[...]
    rgb_t[...] = full.T.astype(jnp.bfloat16)
    rgb_b[pl.ds(0, 128)] = full.astype(jnp.bfloat16)
    rgb_b[pl.ds(128, 128)] = full.astype(jnp.bfloat16)

    spots = lax.broadcasted_iota(jnp.int32, (width, 256), 0)
    right_ok = (col < cols_n - 1).astype(jnp.float32)
    left_ok = (col > 0).astype(jnp.float32)
    wide[...] = jnp.where(
        spots < breadth, 1.0, jnp.where(spots < breadth + WRAP // 2, right_ok, left_ok)
    )
    up_ok = (place > 0).astype(jnp.float32)
    down_ok = (place < ranks - 1).astype(jnp.float32)

    def row_ok(row):
        return jnp.where(row < 0, up_ok, jnp.where(row >= height, down_ok, 1.0))

    lane_half = lax.broadcasted_iota(jnp.int32, (1, 256), 1) < 128

    for_each(DIRS, lambda d: aux_arrival(d).wait_recv())
    target_p[...] = jnp.zeros(target_p.shape, jnp.float32)
    target_t[...] = jnp.zeros(target_t.shape, jnp.float32)
    mask_t[...] = jnp.zeros(mask_t.shape, jnp.float32)
    pairs_two = (height + 4) // 2
    near = lax.broadcasted_iota(jnp.int32, (4, 128), 1) < WRAP // 2
    for r in range(-2, height + 2):
        if r < 0:
            mid, left, right, at = ((-1, 0), (-1, -1), (-1, 1), height + r)
        elif r < height:
            mid, left, right, at = (None, (0, -1), (0, 1), r)
        else:
            mid, left, right, at = ((1, 0), (1, -1), (1, 1), r - height)
        center = aux[:, at, :] if mid is None else aux_in[slot[mid], :, at, :]
        from_left = aux_in[slot[left], :, at, pl.ds(breadth - 128, 128)]
        from_right = aux_in[slot[right], :, at, pl.ds(0, 128)]
        tail = jnp.where(near, from_right, pltpu.roll(from_left, WRAP, 1))
        q, half = divmod(r + 2, 2)
        for part, lanes in ((center, pl.ds(0, breadth)), (tail, pl.ds(breadth, 128))):
            target_p[q, pl.ds(3 * half, 3), lanes] = part[0:3]
            for k in range(3):
                target_p[q, pl.ds(8 + 3 * half + k, 1), lanes] = part[3:4]
    for q in range(pairs_two):
        target_t[q, :, pl.ds(0, 8)] = target_p[q, pl.ds(0, 8)].T[0:width]
        mask_t[q, :, pl.ds(0, 8)] = target_p[q, pl.ds(8, 8)].T[0:width]

    bias_one = jnp.concatenate([bone_ref[...], bone_ref[...]], axis=1)
    bias_two = jnp.concatenate([btwo_ref[...], btwo_ref[...]], axis=1)

    def put(ref, row, value):
        ref[row, :, pl.ds(0, 128)] = pltpu.roll(value, 1, 0).astype(jnp.bfloat16)
        ref[row, :, pl.ds(128, 128)] = value.astype(jnp.bfloat16)
        ref[row, :, pl.ds(256, 128)] = pltpu.roll(value, width - 1, 0).astype(jnp.bfloat16)

    def put_pair(ref, q, value):
        put(ref, 2 * q, value[:, 0:128])
        put(ref, 2 * q + 1, value[:, 128:256])

    def conv(ref, q, which, count):
        window = jnp.concatenate(
            [ref[2 * q + i, pl.ds(0, count), :] for i in range(4)], axis=1
        )
        return jnp.dot(window, weights[which], preferred_element_type=jnp.float32)

    def parts_of(pre):
        turn = 0.5 * jnp.tanh(0.5 * pre)
        return 0.5 + turn, 0.5 - turn

    tail_pick = lax.broadcasted_iota(jnp.int32, (WRAP, 128), 0) < WRAP // 2

    def expand(row, middle, from_left, from_right):
        tail = jnp.where(
            tail_pick, from_right.astype(jnp.float32), from_left.astype(jnp.float32)
        )
        put(zx, row, jnp.concatenate([middle.astype(jnp.float32), tail], axis=0))

    def first_layer(q, product):
        pre = product + bias_one
        sigma, rest = parts_of(pre)
        row = 2 * q - 3
        inside = jnp.where(lane_half, row_ok(row), row_ok(row + 1))
        kept = sigma * (wide[...] * inside)
        hidden = pre * kept
        slope1[q] = kept + hidden * rest
        put_pair(h1, q, hidden)

    def second_layer(q, product):
        pre = product + bias_two
        sigma, rest = parts_of(pre)
        hidden = pre * sigma
        slope = sigma + hidden * rest
        color = jnp.dot(
            hidden.astype(jnp.bfloat16), rgb_t[...], preferred_element_type=jnp.float32
        )
        residual = mask_t[q] * (color - target_t[q])
        coarse = residual.astype(jnp.bfloat16)
        fine = (residual - coarse.astype(jnp.float32)).astype(jnp.bfloat16)
        grad = jnp.dot(
            jnp.concatenate([coarse, fine], axis=1),
            rgb_b[...],
            preferred_element_type=jnp.float32,
        )
        put_pair(g2, q, grad * slope)

    def back_second(q, product):
        put_pair(g1, q, product * slope1[q + 1])

    half = height // 2
    cuts = (
        (lambda q: conv(zx, q, 0, width), first_layer, 2, 1 + half, half + 3),
        (lambda q: conv(h1, q, 1, width), second_layer, 2, half, half + 2),
        (lambda q: conv(g2, q, 3, width), back_second, 2, half - 1, half + 1),
    )

    results = ((z_ref, latent_out), (m_ref, one_out), (v_ref, two_out), (grad_ref, grad_out))

    def leave(k, q):
        rows = pl.ds(2 * q, 2)
        src, dst = results[k]
        return pltpu.make_async_copy(src.at[rows], dst.at[rows], out_sem.at[k, q])

    for step in range(STEPS):
        last = step == STEPS - 1
        for_each(sides, lambda d: halo_arrival(d, step).wait_recv())

        def own_row(r):
            expand(
                r + HALO, stage[step, r], col_in[step, 0, r], col_in[step, 1, r]
            )

        for r in range(height):
            own_row(r)
        for product, finish, low, high, _ in cuts:
            sweep(product, finish, range(low, high))
        for_each(verticals, lambda d: halo_arrival(d, step).wait_recv())

        def halo_row(r):
            expand(r, row_in[step, 0, r], diag_in[step, 0, 0, r], diag_in[step, 0, 1, r])
            expand(
                r + HALO + height,
                row_in[step, 1, r],
                diag_in[step, 1, 0, r],
                diag_in[step, 1, 1, r],
            )

        for r in range(HALO):
            halo_row(r)
        for product, finish, low, high, count in cuts:
            sweep(product, finish, [*range(low), *range(high, count)])

        if step == 0:
            loads[7].wait()
            loads[8].wait()

        for q in range(half):
            grads = conv(g1, q, 2, breadth)
            for i in range(2):
                r = 2 * q + i
                grad = grads[:, 128 * i : 128 * (i + 1)]
                if last:
                    grad_ref[r] = grad
                    continue
                first = BETA_ONE * m_ref[r] + (1.0 - BETA_ONE) * grad
                second = BETA_TWO * v_ref[r] + (1.0 - BETA_TWO) * grad * grad
                fresh = z_ref[r] - LEARN_RATE * first / (jnp.sqrt(second) + EPSILON)
                m_ref[r] = first
                v_ref[r] = second
                z_ref[r] = fresh
                stage[step + 1, r] = fresh.astype(jnp.bfloat16)
            if last:
                leave(3, q).start()
            elif step == STEPS - 2:
                for k in range(3):
                    leave(k, q).start()
            if not last and 2 * (q + 1) == HALO:
                for_each(uppers, lambda d: halo_copy(d, step + 1).start())
        if not last:
            for_each(lowers + sides, lambda d: halo_copy(d, step + 1).start())

    for step in range(STEPS):
        for_each(DIRS, lambda d: halo_copy(d, step).wait_send())
    for_each(DIRS, lambda d: aux_copy(d).wait_send())
    for k in range(4):
        for q in range(half):
            leave(k, q).wait()


def body(
    sizes,
    latent,
    moment_one,
    moment_two,
    hole_mask,
    target_rgb,
    kernel_one,
    bias_one,
    kernel_two,
    bias_two,
    rgb_weight,
):
    height, breadth, channels = latent.shape
    width = breadth + WRAP
    rows_n, cols_n, cores_n = sizes
    f32, bf16 = jnp.float32, jnp.bfloat16
    far = pl.BlockSpec(memory_space=pltpu.HBM)
    near = pl.BlockSpec(memory_space=pltpu.VMEM)
    tile = jax.ShapeDtypeStruct(latent.shape, f32)
    half = height // 2
    scratch = [
        *[pltpu.VMEM((height, breadth, channels), f32)] * 4,
        pltpu.VMEM((height, breadth), jnp.int32),
        pltpu.VMEM((4, height, breadth), f32),
        pltpu.VMEM((8, 4, height, breadth), f32),
        pltpu.VMEM((STEPS, height, breadth, channels), bf16),
        pltpu.VMEM((STEPS, 2, HALO, breadth, channels), bf16),
        pltpu.VMEM((STEPS, 2, height, WRAP, channels), bf16),
        pltpu.VMEM((STEPS, 2, 2, HALO, WRAP, channels), bf16),
        pltpu.VMEM((height + 8, width, 3 * channels), bf16),
        pltpu.VMEM((height + 6, width, 3 * channels), bf16),
        pltpu.VMEM((height + 4, width, 3 * channels), bf16),
        pltpu.VMEM((height + 2, width, 3 * channels), bf16),
        pltpu.VMEM((half + 3, width, 2 * channels), f32),
        pltpu.VMEM((4, 12 * channels, 2 * channels), bf16),
        pltpu.VMEM((width, 2 * channels), f32),
        pltpu.VMEM((128, 2 * channels), f32),
        pltpu.VMEM((2 * channels, 128), bf16),
        pltpu.VMEM((256, 2 * channels), bf16),
        pltpu.VMEM((half + 2, 16, breadth + 128), f32),
        pltpu.VMEM((half + 2, width, 128), f32),
        pltpu.VMEM((half + 2, width, 128), f32),
        pltpu.SemaphoreType.DMA((9,)),
        pltpu.SemaphoreType.DMA((4, half)),
        pltpu.SemaphoreType.DMA((STEPS, 8)),
        pltpu.SemaphoreType.DMA((STEPS, 8)),
        pltpu.SemaphoreType.DMA((8,)),
        pltpu.SemaphoreType.DMA((8,)),
    ]
    current, first, second, grad = pl.pallas_call(
        functools.partial(kernel, height, breadth, rows_n, cols_n, cores_n),
        out_shape=(tile, tile, tile, tile),
        in_specs=[far] * 7 + [near] * 3,
        out_specs=(far, far, far, far),
        scratch_shapes=scratch,
        compiler_params=pltpu.CompilerParams(
            collective_id=0, has_side_effects=True, vmem_limit_bytes=60 * 1024 * 1024
        ),
        name="inpaint",
    )(
        latent,
        moment_one,
        moment_two,
        hole_mask,
        target_rgb,
        kernel_one.reshape(9 * channels, channels),
        kernel_two.reshape(9 * channels, channels),
        bias_one.reshape(1, channels),
        bias_two.reshape(1, channels),
        rgb_weight,
    )
    first = BETA_ONE * first + (1.0 - BETA_ONE) * grad
    second = BETA_TWO * second + (1.0 - BETA_TWO) * grad * grad
    current = current - LEARN_RATE * first / (jnp.sqrt(second) + EPSILON)
    return current, first, second


def solution(mesh):
    sizes = (mesh.shape["row"], mesh.shape["col"], mesh.shape["cores"])
    tile = P(("parts", "row", "cores"), "col", None)
    return jax.shard_map(
        functools.partial(body, sizes),
        mesh=mesh,
        in_specs=(
            tile,
            tile,
            tile,
            P(("parts", "row", "cores"), "col"),
            P(None, ("parts", "row", "cores"), "col"),
            P(),
            P(),
            P(),
            P(),
            P(),
        ),
        out_specs=(tile, tile, tile),
        check_vma=False,
    )
```

profile of v0, /device:TPU:0, one launch (start us, length us, event | category | flops | bytes accessed | tf_op | source)
XLA Modules:
  0.0 28.1 jit_solution(9545277721909855743)
XLA Ops:
  0.6 24.6 %inpaint.1 = (f32[8,128,128]{2,1,0:T(8,128)}, f32[8,128,128]{2,1,0:T(8,128)}, f32[8,128,128]{2,1,0:T(8,128)}, f32[8,128,128]{2,1,0:T(8,128)}) custom-call(f32[8,128,128]{2,1,0:T(8,128)} %latent_hbm.1, f32[8,128,128]{2,1,0:T(8,128)} %one_hbm.1, f32[8,128,128]{2,1,0:T(8,128)} %two_hbm.1, s32[8,128]{1,0:T(8,128)} %mask_hbm.1, f32[3,8,128]{2,1,0:T(8,128)} %target_hbm.1, ...), custom_call_target="tpu_custom_call" | custom-call | tf_op jit(solution)/shard_map/inpaint/pallas_call | solution.py:489
  25.3 2.8 %divide_subtract_fusion = (f32[8,128,128]{2,1,0:T(8,128)}, f32[8,128,128]{2,1,0:T(8,128)}, f32[8,128,128]{2,1,0:T(8,128)}) fusion(f32[8,128,128]{2,1,0:T(8,128)} %get-tuple-element.7, f32[8,128,128]{2,1,0:T(8,128)} %get-tuple-element.9, f32[8,128,128]{2,1,0:T(8,128)} %get-tuple-element.8, f32[8,128,128]{2,1,0:T(8,128)} %get-tuple-element.10), kind=kLoop, calls=%fused_computation.2 | loop fusion | flops 1441792 | bytes 3670016 | tf_op jit(solution)/shard_map/sub | solution.py:513
where the time goes:
time: 28.3 us; the launch traced here: 28.1 us
  Pallas kernels  24.6 us (87%)
  other arithmetic  2.83 us (10%)
  between operations  0.64 us (2%)
    pallas_call x1, Pallas kernels, body(): pl.pallas_call(functools.partial(kernel, height, breadth, rows_n, cols_n,...  24.6 us
    sub x1, other arithmetic, body(): current = current - LEARN_RATE * first / (jnp.sqrt(second) + EPSILON)  2.83 us

commit v1 on v0

--- a/solution.py
+++ b/solution.py
@@ -19,13 +19,45 @@
 DIRS = [(-1, 0), (1, 0), (0, -1), (0, 1), (-1, -1), (-1, 1), (1, -1), (1, 1)]
 
 
-def sweep(product, finish, places):
-    ready = product(places[0])
-    for at, q in enumerate(places):
-        held = ready
-        if at + 1 < len(places):
-            ready = product(places[at + 1])
-        finish(q, held)
+def sweep(tasks):
+    ready = None
+    for at, (product, finish, places) in enumerate(tasks):
+        held = product(places) if at == 0 else ready
+        if at + 1 < len(tasks):
+            ready = tasks[at + 1][0](tasks[at + 1][2])
+        finish(places, held)
+
+
+def renew(first, second, current, grad):
+    first = BETA_ONE * first + (1.0 - BETA_ONE) * grad
+    second = BETA_TWO * second + (1.0 - BETA_TWO) * grad * grad
+    return first, second, current - LEARN_RATE * first / (jnp.sqrt(second) + EPSILON)
+
+
+def last_update(half, z_in, m_in, v_in, g_in, z_out, m_out, v_out, z, m, v, g, in_sem, out_sem):
+    sources = ((z_in, z), (m_in, m), (v_in, v), (g_in, g))
+    targets = ((z, z_out), (m, m_out), (v, v_out))
+
+    def moves(pairs, sem, q):
+        rows = pl.ds(2 * q, 2)
+        return [
+            pltpu.make_async_copy(src.at[rows], dst.at[rows], sem.at[k, q])
+            for k, (src, dst) in enumerate(pairs)
+        ]
+
+    for q in range(half):
+        for c in moves(sources, in_sem, q):
+            c.start()
+    for q in range(half):
+        for c in moves(sources, in_sem, q):
+            c.wait()
+        rows = pl.ds(2 * q, 2)
+        m[rows], v[rows], z[rows] = renew(m[rows], v[rows], z[rows], g[rows])
+        for c in moves(targets, out_sem, q):
+            c.start()
+    for q in range(half):
+        for c in moves(targets, out_sem, q):
+            c.wait()
 
 
 def kernel(
@@ -307,9 +339,13 @@
         put(ref, 2 * q, value[:, 0:128])
         put(ref, 2 * q + 1, value[:, 128:256])
 
-    def conv(ref, q, which, count):
+    def conv(ref, which, count, places):
         window = jnp.concatenate(
-            [ref[2 * q + i, pl.ds(0, count), :] for i in range(4)], axis=1
+            [
+                jnp.concatenate([ref[2 * q + i, pl.ds(0, count), :] for i in range(4)], axis=1)
+                for q in places
+            ],
+            axis=0,
         )
         return jnp.dot(window, weights[which], preferred_element_type=jnp.float32)
 
@@ -325,42 +361,55 @@
         )
         put(zx, row, jnp.concatenate([middle.astype(jnp.float32), tail], axis=0))
 
-    def first_layer(q, product):
-        pre = product + bias_one
-        sigma, rest = parts_of(pre)
-        row = 2 * q - 3
-        inside = jnp.where(lane_half, row_ok(row), row_ok(row + 1))
-        kept = sigma * (wide[...] * inside)
-        hidden = pre * kept
-        slope1[q] = kept + hidden * rest
-        put_pair(h1, q, hidden)
-
-    def second_layer(q, product):
-        pre = product + bias_two
-        sigma, rest = parts_of(pre)
-        hidden = pre * sigma
-        slope = sigma + hidden * rest
+    def split(value, count, n):
+        return [value[count * i : count * (i + 1)] for i in range(n)]
+
+    def first_layer(places, product):
+        for q, part in zip(places, split(product, width, len(places))):
+            pre = part + bias_one
+            sigma, rest = parts_of(pre)
+            row = 2 * q - 3
+            inside = wide[...]
+            if row < 0 or row + 1 >= height:
+                inside = inside * jnp.where(lane_half, row_ok(row), row_ok(row + 1))
+            kept = sigma * inside
+            hidden = pre * kept
+            slope1[q] = kept + hidden * rest
+            put_pair(h1, q, hidden)
+
+    def second_layer(places, product):
+        n = len(places)
+        rounded, slopes = [], []
+        for part in split(product, width, n):
+            pre = part + bias_two
+            sigma, rest = parts_of(pre)
+            hidden = pre * sigma
+            slopes.append(sigma + hidden * rest)
+            rounded.append(hidden.astype(jnp.bfloat16))
         color = jnp.dot(
-            hidden.astype(jnp.bfloat16), rgb_t[...], preferred_element_type=jnp.float32
-        )
-        residual = mask_t[q] * (color - target_t[q])
-        coarse = residual.astype(jnp.bfloat16)
-        fine = (residual - coarse.astype(jnp.float32)).astype(jnp.bfloat16)
+            jnp.concatenate(rounded, axis=0), rgb_t[...], preferred_element_type=jnp.float32
+        )
+        terms = []
+        for q, part in zip(places, split(color, width, n)):
+            residual = mask_t[q] * (part - target_t[q])
+            coarse = residual.astype(jnp.bfloat16)
+            fine = (residual - coarse.astype(jnp.float32)).astype(jnp.bfloat16)
+            terms.append(jnp.concatenate([coarse, fine], axis=1))
         grad = jnp.dot(
-            jnp.concatenate([coarse, fine], axis=1),
-            rgb_b[...],
-            preferred_element_type=jnp.float32,
-        )
-        put_pair(g2, q, grad * slope)
-
-    def back_second(q, product):
-        put_pair(g1, q, product * slope1[q + 1])
+            jnp.concatenate(terms, axis=0), rgb_b[...], preferred_element_type=jnp.float32
+        )
+        for q, part, slope in zip(places, split(grad, width, n), slopes):
+            put_pair(g2, q, part * slope)
+
+    def back_second(places, product):
+        for q, part in zip(places, split(product, width, len(places))):
+            put_pair(g1, q, part * slope1[q + 1])
 
     half = height // 2
-    cuts = (
-        (lambda q: conv(zx, q, 0, width), first_layer, 2, 1 + half, half + 3),
-        (lambda q: conv(h1, q, 1, width), second_layer, 2, half, half + 2),
-        (lambda q: conv(g2, q, 3, width), back_second, 2, half - 1, half + 1),
+    stages = (
+        (functools.partial(conv, zx, 0, width), first_layer, half + 3, 1 + half),
+        (functools.partial(conv, h1, 1, width), second_layer, half + 2, half),
+        (functools.partial(conv, g2, 3, width), back_second, half + 1, half - 1),
     )
 
     results = ((z_ref, latent_out), (m_ref, one_out), (v_ref, two_out), (grad_ref, grad_out))
@@ -381,8 +430,13 @@
 
         for r in range(height):
             own_row(r)
-        for product, finish, low, high, _ in cuts:
-            sweep(product, finish, range(low, high))
+        tasks = []
+        for p, f, _, high in stages[:2]:
+            tasks.append((p, f, list(range(2, high - 1))))
+            tasks.append((p, f, [high - 1]))
+        sweep(tasks)
+        p, f, _, high = stages[2]
+        sweep([(p, f, list(range(2, high)))])
         for_each(verticals, lambda d: halo_arrival(d, step).wait_recv())
 
         def halo_row(r):
@@ -396,37 +450,39 @@
 
         for r in range(HALO):
             halo_row(r)
-        for product, finish, low, high, count in cuts:
-            sweep(product, finish, [*range(low), *range(high, count)])
-
         if step == 0:
             loads[7].wait()
             loads[8].wait()
 
-        for q in range(half):
-            grads = conv(g1, q, 2, breadth)
-            for i in range(2):
-                r = 2 * q + i
-                grad = grads[:, 128 * i : 128 * (i + 1)]
+        def update(places, product):
+            for q, grads in zip(places, split(product, breadth, len(places))):
+                for i in range(2):
+                    r = 2 * q + i
+                    grad = grads[:, 128 * i : 128 * (i + 1)]
+                    if last:
+                        grad_ref[r] = grad
+                        continue
+                    m_ref[r], v_ref[r], z_ref[r] = renew(m_ref[r], v_ref[r], z_ref[r], grad)
+                    stage[step + 1, r] = z_ref[r].astype(jnp.bfloat16)
                 if last:
-                    grad_ref[r] = grad
-                    continue
-                first = BETA_ONE * m_ref[r] + (1.0 - BETA_ONE) * grad
-                second = BETA_TWO * v_ref[r] + (1.0 - BETA_TWO) * grad * grad
-                fresh = z_ref[r] - LEARN_RATE * first / (jnp.sqrt(second) + EPSILON)
-                m_ref[r] = first
-                v_ref[r] = second
-                z_ref[r] = fresh
-                stage[step + 1, r] = fresh.astype(jnp.bfloat16)
-            if last:
-                leave(3, q).start()
-            elif step == STEPS - 2:
-                for k in range(3):
-                    leave(k, q).start()
-            if not last and 2 * (q + 1) == HALO:
-                for_each(uppers, lambda d: halo_copy(d, step + 1).start())
-        if not last:
-            for_each(lowers + sides, lambda d: halo_copy(d, step + 1).start())
+                    leave(3, q).start()
+                elif step == STEPS - 2:
+                    for k in range(3):
+                        leave(k, q).start()
+            if not last:
+                if places[0] == 0:
+                    for_each(uppers, lambda d: halo_copy(d, step + 1).start())
+                if places[-1] == half - 1:
+                    for_each(lowers + sides, lambda d: halo_copy(d, step + 1).start())
+
+        tasks = []
+        for p, f, count, high in stages:
+            tasks.append((p, f, [0, 1]))
+            tasks.append((p, f, list(range(high, count))))
+        last_conv = functools.partial(conv, g1, 2, breadth)
+        tasks.append((last_conv, update, list(range(half // 2))))
+        tasks.append((last_conv, update, list(range(half // 2, half))))
+        sweep(tasks)
 
     for step in range(STEPS):
         for_each(DIRS, lambda d: halo_copy(d, step).wait_send())
@@ -508,10 +564,19 @@
         bias_two.reshape(1, channels),
         rgb_weight,
     )
-    first = BETA_ONE * first + (1.0 - BETA_ONE) * grad
-    second = BETA_TWO * second + (1.0 - BETA_TWO) * grad * grad
-    current = current - LEARN_RATE * first / (jnp.sqrt(second) + EPSILON)
-    return current, first, second
+    return pl.pallas_call(
+        functools.partial(last_update, half),
+        out_shape=(tile, tile, tile),
+        in_specs=[far] * 4,
+        out_specs=(far, far, far),
+        scratch_shapes=[
+            *[pltpu.VMEM((height, breadth, channels), f32)] * 4,
+            pltpu.SemaphoreType.DMA((4, half)),
+            pltpu.SemaphoreType.DMA((3, half)),
+        ],
+        compiler_params=pltpu.CompilerParams(vmem_limit_bytes=60 * 1024 * 1024),
+        name="last_update",
+    )(current, first, second, grad)
 
 
 def solution(mesh):

time: 28.3 us -> 26.8 us (0.947)
  other arithmetic: 2.83 us -> 0 us
  Pallas kernels: 24.6 us -> 25.9 us
    sub x1 -> x0, other arithmetic: 2.83 us -> none  [body(): current = current - LEARN_RATE * first / (jnp.sqrt(second) + EPSILON)]
    pallas_call x0 -> x1, Pallas kernels: none -> 2.68 us  [body(): pl.pallas_call(functools.partial(last_update, half), out_shape=(tile, til...]
    pallas_call x1, Pallas kernels: 24.6 us -> 23.2 us  [body(): pl.pallas_call(functools.partial(kernel, height, breadth, rows_n, cols_n,...]
where the time goes in v1:
time: 26.8 us; the launch traced here: 26.6 us
  Pallas kernels  25.9 us (97%)
  between operations  0.64 us (2%)
    pallas_call x1, Pallas kernels, body(): pl.pallas_call(functools.partial(kernel, height, breadth, rows_n, cols_n,...  23.2 us
    pallas_call x1, Pallas kernels, body(): pl.pallas_call(functools.partial(last_update, half), out_shape=(tile, til...  2.68 us

profile of v1, /device:TPU:0, one launch (start us, length us, event | category | flops | bytes accessed | tf_op | source)
XLA Modules:
  0.0 26.6 jit_solution(11638791177287059632)
XLA Ops:
  0.6 23.2 %inpaint.1 = (f32[8,128,128]{2,1,0:T(8,128)}, f32[8,128,128]{2,1,0:T(8,128)}, f32[8,128,128]{2,1,0:T(8,128)}, f32[8,128,128]{2,1,0:T(8,128)}) custom-call(f32[8,128,128]{2,1,0:T(8,128)} %latent_hbm.1, f32[8,128,128]{2,1,0:T(8,128)} %one_hbm.1, f32[8,128,128]{2,1,0:T(8,128)} %two_hbm.1, s32[8,128]{1,0:T(8,128)} %mask_hbm.1, f32[3,8,128]{2,1,0:T(8,128)} %target_hbm.1, ...), custom_call_target="tpu_custom_call" | custom-call | tf_op jit(solution)/shard_map/inpaint/pallas_call | solution.py:545
  23.9 2.7 %last_update.1 = (f32[8,128,128]{2,1,0:T(8,128)}, f32[8,128,128]{2,1,0:T(8,128)}, f32[8,128,128]{2,1,0:T(8,128)}) custom-call(f32[8,128,128]{2,1,0:T(8,128)} %get-tuple-element.7.z_in, f32[8,128,128]{2,1,0:T(8,128)} %get-tuple-element.8.m_in, f32[8,128,128]{2,1,0:T(8,128)} %get-tuple-element.9.v_in, f32[8,128,128]{2,1,0:T(8,128)} %get-tuple-element.10.g_in), custom_call_target="tpu_custom_call" | custom-call | tf_op jit(solution)/shard_map/last_update/pallas_call | solution.py:567

commit v2 on v1

--- a/solution.py
+++ b/solution.py
@@ -147,14 +147,12 @@
         local(latent_hbm, z_ref, 0),
         local(target_hbm, aux.at[pl.ds(0, 3)], 1),
         local(mask_hbm, maski, 2),
-        local(ktwo_hbm, weights.at[1, pl.ds(0, 9 * 128), pl.ds(0, 128)], 3),
-        local(kone_hbm, weights.at[0, pl.ds(0, 9 * 128), pl.ds(0, 128)], 4),
-        local(kone_hbm, weights.at[0, pl.ds(384, 9 * 128), pl.ds(128, 128)], 5),
-        local(ktwo_hbm, weights.at[1, pl.ds(384, 9 * 128), pl.ds(128, 128)], 6),
-        local(one_hbm, m_ref, 7),
-        local(two_hbm, v_ref, 8),
+        local(kone_hbm, weights.at[0, pl.ds(0, 9 * 128), pl.ds(0, 128)], 3),
+        local(ktwo_hbm, weights.at[1, pl.ds(0, 9 * 128), pl.ds(0, 128)], 4),
+        local(one_hbm, m_ref, 5),
+        local(two_hbm, v_ref, 6),
     ]
-    for c in loads:
+    for c in loads[:5]:
         c.start()
 
     barrier = pltpu.get_barrier_semaphore()
@@ -257,26 +255,29 @@
     aux[3] = maski[...].astype(jnp.float32)
     for_each(DIRS, lambda d: aux_copy(d).start())
 
+    loads[3].wait()
+    loads[4].wait()
+    loads[5].start()
+    loads[6].start()
+    for_each(DIRS, lambda d: aux_arrival(d).wait_recv())
+    for_each(sides, lambda d: halo_arrival(d, 0).wait_recv())
+
     zero_block = jnp.zeros((384, 128), jnp.bfloat16)
     for i in range(4):
         weights[i, pl.ds(9 * 128, 384), pl.ds(0, 128)] = zero_block
         weights[i, pl.ds(0, 384), pl.ds(128, 128)] = zero_block
-    for i in range(3, 7):
-        loads[i].wait()
-
-    def turned(layer):
-        def flip(tap, carry):
-            block = weights[layer, pl.ds(pl.multiple_of(tap * 128, 128), 128), pl.ds(0, 128)]
+    for layer in range(2):
+        weights[layer, pl.ds(384, 9 * 128), pl.ds(128, 128)] = weights[
+            layer, pl.ds(0, 9 * 128), pl.ds(0, 128)
+        ]
+
+    for layer in (1, 0):
+        for tap in range(9):
+            block = weights[layer, pl.ds(tap * 128, 128), pl.ds(0, 128)]
             block = block.astype(jnp.float32).T.astype(jnp.bfloat16)
-            spot = pl.multiple_of((8 - tap) * 128, 128)
+            spot = (8 - tap) * 128
             weights[2 + layer, pl.ds(spot, 128), pl.ds(0, 128)] = block
-            weights[2 + layer, pl.ds(pl.multiple_of(spot + 384, 128), 128), pl.ds(128, 128)] = block
-            return carry
-
-        lax.fori_loop(0, 9, flip, 0)
-
-    turned(1)
-    turned(0)
+            weights[2 + layer, pl.ds(spot + 384, 128), pl.ds(128, 128)] = block
 
     rgb_f[...] = jnp.zeros(rgb_f.shape, jnp.float32)
     projection = rgb_ref[...].astype(jnp.float32)
@@ -301,7 +302,6 @@
 
     lane_half = lax.broadcasted_iota(jnp.int32, (1, 256), 1) < 128
 
-    for_each(DIRS, lambda d: aux_arrival(d).wait_recv())
     target_p[...] = jnp.zeros(target_p.shape, jnp.float32)
     target_t[...] = jnp.zeros(target_t.shape, jnp.float32)
     mask_t[...] = jnp.zeros(mask_t.shape, jnp.float32)
@@ -421,7 +421,8 @@
 
     for step in range(STEPS):
         last = step == STEPS - 1
-        for_each(sides, lambda d: halo_arrival(d, step).wait_recv())
+        if step > 0:
+            for_each(sides, lambda d: halo_arrival(d, step).wait_recv())
 
         def own_row(r):
             expand(
@@ -451,8 +452,8 @@
         for r in range(HALO):
             halo_row(r)
         if step == 0:
-            loads[7].wait()
-            loads[8].wait()
+            loads[5].wait()
+            loads[6].wait()
 
         def update(places, product):
             for q, grads in zip(places, split(product, breadth, len(places))):
@@ -535,7 +536,7 @@
         pltpu.VMEM((half + 2, 16, breadth + 128), f32),
         pltpu.VMEM((half + 2, width, 128), f32),
         pltpu.VMEM((half + 2, width, 128), f32),
-        pltpu.SemaphoreType.DMA((9,)),
+        pltpu.SemaphoreType.DMA((7,)),
         pltpu.SemaphoreType.DMA((4, half)),
         pltpu.SemaphoreType.DMA((STEPS, 8)),
         pltpu.SemaphoreType.DMA((STEPS, 8)),

time: 26.8 us -> 26.6 us (level)
  no operation moved by 1% of the time
where the time goes in v2:
time: 26.6 us; the launch traced here: 26.4 us
  Pallas kernels  25.8 us (97%)
  between operations  0.64 us (2%)
    pallas_call x1, Pallas kernels, body(): pl.pallas_call(functools.partial(kernel, height, breadth, rows_n, cols_n,...  23.1 us
    pallas_call x1, Pallas kernels, body(): pl.pallas_call(functools.partial(last_update, half), out_shape=(tile, til...  2.68 us

profile of v2, /device:TPU:0, one launch (start us, length us, event | category | flops | bytes accessed | tf_op | source)
XLA Modules:
  0.0 26.4 jit_solution(8925596287043653782)
XLA Ops:
  0.6 23.1 %inpaint.1 = (f32[8,128,128]{2,1,0:T(8,128)}, f32[8,128,128]{2,1,0:T(8,128)}, f32[8,128,128]{2,1,0:T(8,128)}, f32[8,128,128]{2,1,0:T(8,128)}) custom-call(f32[8,128,128]{2,1,0:T(8,128)} %latent_hbm.1, f32[8,128,128]{2,1,0:T(8,128)} %one_hbm.1, f32[8,128,128]{2,1,0:T(8,128)} %two_hbm.1, s32[8,128]{1,0:T(8,128)} %mask_hbm.1, f32[3,8,128]{2,1,0:T(8,128)} %target_hbm.1, ...), custom_call_target="tpu_custom_call" | custom-call | tf_op jit(solution)/shard_map/inpaint/pallas_call | solution.py:546
  23.7 2.7 %last_update.1 = (f32[8,128,128]{2,1,0:T(8,128)}, f32[8,128,128]{2,1,0:T(8,128)}, f32[8,128,128]{2,1,0:T(8,128)}) custom-call(f32[8,128,128]{2,1,0:T(8,128)} %get-tuple-element.7.z_in, f32[8,128,128]{2,1,0:T(8,128)} %get-tuple-element.8.m_in, f32[8,128,128]{2,1,0:T(8,128)} %get-tuple-element.9.v_in, f32[8,128,128]{2,1,0:T(8,128)} %get-tuple-element.10.g_in), custom_call_target="tpu_custom_call" | custom-call | tf_op jit(solution)/shard_map/last_update/pallas_call | solution.py:568
